TPU v7x, 32 devices: a whole 2x2x4 slice. The times are simulated.
32 devices in a mesh: groups: 2 (over y), seq: 8 (over z, x), head: 2 (over core).
Axes of the slice: x: 2, y: 2, z: 4, core: 2. Of those that a mesh axis runs over, the one named last changes fastest.
Arguments:
- queries: bfloat16 [8192, 8192], P(('groups', 'seq'), 'head'), parts along dimension 0, may hold values from -32 to 32
- keys: bfloat16 [8192, 1024], P(('groups', 'seq'), 'head'), parts along dimension 0, may hold values from -32 to 32
- values: bfloat16 [8192, 1024], P(('groups', 'seq'), 'head'), parts along dimension 0, may hold values from -6 to 6
- block_lists: int32 [8, 128, 20], P('head', 'groups'), parts along dimension 1, may hold values from -1 to 63, as said below
- dec_queries: bfloat16 [512, 2, 8192], P(('groups', 'seq'), None, 'head'), parts along dimension 0, may hold values from -40 to 40
- dec_keys: bfloat16 [512, 2, 1024], P(('groups', 'seq'), None, 'head'), parts along dimension 0, may hold values from -40 to 40
- decode_value_rows: bfloat16 [512, 2, 1024], P(('groups', 'seq'), None, 'head'), parts along dimension 0, may hold values from -6 to 6
- positions: int32 [512], P('groups'), parts along dimension 0, may hold values from 2048 to 4096
Outputs:
- prompt_out: bfloat16 [8192, 8192], P(('groups', 'seq'), 'head'), parts along dimension 0
- decode_out: bfloat16 [512, 2, 8192], P(('groups', 'seq'), None, 'head'), parts along dimension 0
There are 2 independent parts, one for each index of `groups`. A program takes and returns all parts, laid end to end along the dimension named above; each array names one. Nothing has to cross between parts.
Inputs may be any that keep to these rules, and one draw needn't show every extreme that they name: In each row block_lists[h, b] the entries are distinct, entries -1 stand after all others, the first entry is b, and every entry is at most b. For each h the entries smaller than their row's b - 3 take exactly 16 distinct values.
All inputs are finite; a program needn't handle non-finite values.
Results may differ from a plain program's by a relative error of at most 0.0041.
Values may be sent and summed in bfloat16 or wider, within the bound.
No kernel may reach another device: no remote copies, remote signals or barrier semaphores. Data moves between devices by JAX's collectives and lax.ppermute only.
A program may use at most 192 MiB of HBM per device.

v0:
```python
import math

import jax
import jax.numpy as jnp
from jax import lax
from jax.sharding import PartitionSpec as P

QUERY_HEADS = 64
KEY_VALUE_HEADS = 8
HEAD_SIZE = 128
BLOCK_POSITIONS = 64
DECODE_STEPS = 2


def block_mask(entries, qblock, width):
    keypos = (
        entries[:, :, None] * width + jnp.arange(width, dtype=jnp.int32)[None, None, :]
    ).reshape(entries.shape[0], -1)
    valid = jnp.repeat(entries >= 0, width, axis=1)
    qpos = qblock * width + jnp.arange(width, dtype=jnp.int32)
    return valid[:, None, :] & (keypos[:, None, :] <= qpos[None, :, None])


def attend_tile(query_tile, key_matrix, value_matrix, allowed, scale):
    scores = (
        jnp.einsum("rhgd,hsd->hgrs", query_tile, key_matrix, preferred_element_type=jnp.float32)
        * scale
    )
    scores = jnp.where(allowed[:, None], scores, -1e30)
    top = jnp.max(scores, axis=-1, keepdims=True)
    weights = jnp.exp(scores - top)
    total = jnp.sum(weights, axis=-1)
    mixed = jnp.einsum(
        "hgrs,hsd->hgrd",
        weights.astype(jnp.bfloat16),
        value_matrix,
        preferred_element_type=jnp.float32,
    )
    mixed = mixed / total[..., None]
    return mixed.transpose(2, 0, 1, 3).astype(jnp.bfloat16)


def local(queries, keys, values, block_lists, dec_queries, dec_keys, decode_value_rows, positions):
    rows = queries.shape[0]
    kv_heads = keys.shape[1] // HEAD_SIZE
    head_group = QUERY_HEADS // KEY_VALUE_HEADS
    scale = 1.0 / math.sqrt(HEAD_SIZE)
    per_dev = rows // BLOCK_POSITIONS
    blocks_all = block_lists.shape[1]
    me = lax.axis_index("seq")
    first = me * per_dev
    mine = lax.dynamic_slice_in_dim(block_lists, first, per_dev, 1)
    key_all, value_all = (
        lax.all_gather(keys, "seq", axis=0, tiled=True),
        lax.all_gather(values, "seq", axis=0, tiled=True),
    )
    key_pool = key_all.reshape(blocks_all, BLOCK_POSITIONS, kv_heads, HEAD_SIZE).transpose(
        2, 0, 1, 3
    )
    value_pool = value_all.reshape(blocks_all, BLOCK_POSITIONS, kv_heads, HEAD_SIZE).transpose(
        2, 0, 1, 3
    )
    cache_slots = jnp.maximum(mine, 0)
    head_index = jnp.arange(kv_heads, dtype=jnp.int32)[None, :, None]
    slot_order = cache_slots.transpose(1, 0, 2)
    key_matrix = key_pool[head_index, slot_order]
    value_matrix = value_pool[head_index, slot_order]
    blocked_queries = queries.reshape(per_dev, BLOCK_POSITIONS, kv_heads, head_group, HEAD_SIZE)

    def prompt_tile(item):
        tile, krows, vrows, entries, index = item
        allowed = block_mask(entries, index, BLOCK_POSITIONS)
        return attend_tile(
            tile,
            krows.reshape(kv_heads, -1, HEAD_SIZE),
            vrows.reshape(kv_heads, -1, HEAD_SIZE),
            allowed,
            scale,
        )

    tile_ids = first + jnp.arange(per_dev, dtype=jnp.int32)
    prompt_out = lax.map(
        prompt_tile, (blocked_queries, key_matrix, value_matrix, mine.transpose(1, 0, 2), tile_ids)
    )
    prompt_out = prompt_out.reshape(rows, kv_heads * head_group * HEAD_SIZE)
    owned = dec_queries.shape[0]
    all_queries, all_keys, all_values = (
        lax.all_gather(dec_queries, "seq", axis=0, tiled=True),
        lax.all_gather(dec_keys, "seq", axis=0, tiled=True),
        lax.all_gather(decode_value_rows, "seq", axis=0, tiled=True),
    )
    total_rollouts = all_queries.shape[0]
    cache_pos = first * BLOCK_POSITIONS + jnp.arange(rows, dtype=jnp.int32)
    live = cache_pos[None, :] < positions[:, None]
    cached_key_rows = keys.reshape(rows, kv_heads, HEAD_SIZE)
    cached_value_rows = values.reshape(rows, kv_heads, HEAD_SIZE)
    ownership = (jnp.arange(total_rollouts, dtype=jnp.int32) // owned == me).astype(jnp.float32)
    results = []
    for step in range(DECODE_STEPS):
        heads_of_query = all_queries[:, step].reshape(
            total_rollouts, kv_heads, head_group, HEAD_SIZE
        )
        cache_scores = (
            jnp.einsum(
                "thgd,lhd->thgl",
                heads_of_query,
                cached_key_rows,
                preferred_element_type=jnp.float32,
            )
            * scale
        )
        cache_scores = jnp.where(live[:, None, None, :], cache_scores, -1e30)
        cache_top = lax.pmax(jnp.max(cache_scores, axis=-1), "seq")
        latest_keys = all_keys[:, : step + 1].reshape(total_rollouts, step + 1, kv_heads, HEAD_SIZE)
        latest_values = all_values[:, : step + 1].reshape(
            total_rollouts, step + 1, kv_heads, HEAD_SIZE
        )
        new_scores = (
            jnp.einsum(
                "thgd,tshd->thgs", heads_of_query, latest_keys, preferred_element_type=jnp.float32
            )
            * scale
        )
        top = jnp.maximum(cache_top, jnp.max(new_scores, axis=-1))
        cache_weights = jnp.exp(cache_scores - top[..., None])
        new_weights = jnp.exp(new_scores - top[..., None])
        mixed = jnp.einsum(
            "thgl,lhd->thgd",
            cache_weights.astype(jnp.bfloat16),
            cached_value_rows,
            preferred_element_type=jnp.float32,
        )
        fresh_mixed = jnp.einsum(
            "thgs,tshd->thgd",
            new_weights.astype(jnp.bfloat16),
            latest_values,
            preferred_element_type=jnp.float32,
        )
        mixed = mixed + ownership[:, None, None, None] * fresh_mixed
        totals = jnp.sum(cache_weights, axis=-1) + ownership[:, None, None] * jnp.sum(
            new_weights, axis=-1
        )
        mixed, totals = lax.psum((mixed, totals), "seq")
        mixed = lax.dynamic_slice_in_dim(mixed, me * owned, owned, 0)
        totals = lax.dynamic_slice_in_dim(totals, me * owned, owned, 0)
        results.append(
            (mixed / totals[..., None])
            .astype(jnp.bfloat16)
            .reshape(owned, kv_heads * head_group * HEAD_SIZE)
        )
    decode_out = jnp.stack(results, 1)
    return (prompt_out, decode_out)


def solution(mesh):
    return jax.shard_map(
        local,
        mesh=mesh,
        in_specs=(
            P(("groups", "seq"), "head"),
            P(("groups", "seq"), "head"),
            P(("groups", "seq"), "head"),
            P("head", "groups", None),
            P(("groups", "seq"), None, "head"),
            P(("groups", "seq"), None, "head"),
            P(("groups", "seq"), None, "head"),
            P("groups"),
        ),
        out_specs=(P(("groups", "seq"), "head"), P(("groups", "seq"), None, "head")),
        check_vma=False,
    )
```

profile of v0, /device:TPU:0, one launch (start us, length us, event | category | flops | bytes accessed | tf_op | source)
XLA Modules:
  0.0 615.5 jit_solution(13734063270281315172)
XLA Ops:
  10.6 2.0 reshape.168
  12.6 35.0 %all_gather.18 = bf16[256,2,512]{2,1,0:T(2,128)(2,1)S(1)} all-gather(bf16[32,2,512]{2,1,0:T(2,128)(2,1)} %param.15), channel_id=1, replica_groups=mesh['groups'=2,'seq'=8,'head'=2] {'seq'}, dimensions={0}, use_global_device_ids=true | all-gather | bytes 589824 | tf_op jit(solution)/shard_map/all_gather | solution.py:89
  50.2 32.6 %all_gather.19 = bf16[256,2,512]{2,1,0:T(2,128)(2,1)S(1)} all-gather(bf16[32,2,512]{2,1,0:T(2,128)(2,1)S(1)} %copy-done.5), channel_id=1, replica_groups=mesh['groups'=2,'seq'=8,'head'=2] {'seq'}, dimensions={0}, use_global_device_ids=true | all-gather | bytes 589824 | tf_op jit(solution)/shard_map/all_gather | solution.py:90
  84.4 5.7 copy.152
  90.3 7.3 %all-gather.8.cloned.1.call-done = bf16[256,2,4096]{2,1,0:T(2,128)(2,1)} async-done(((bf16[32,2,4096]{2,1,0:T(2,128)(2,1)}), bf16[256,2,4096]{2,1,0:T(2,128)(2,1)}) %all-gather.8.cloned.1.call-update) | async-done | bytes 4194320 | tf_op jit(solution)/shard_map/all_gather | solution.py:88
  97.6 11.8 %fusion.53 = (bf16[256,1,4096]{2,1,0:T(2,128)(2,1)}, bf16[256,1,4096]{2,1,0:T(2,128)(2,1)}) fusion(bf16[256,2,4096]{2,1,0:T(2,128)(2,1)} %all-gather.8.cloned.1.call-done), kind=kLoop, calls=%fused_computation.87 | loop fusion | bytes 8388608 | tf_op jit(solution)/shard_map/slice | solution.py:100
  109.3 9.3 %copy.149 = bf16[256,1,4096]{0,2,1:T(8,128)(2,1)S(1)} copy(bf16[256,1,4096]{2,1,0:T(2,128)(2,1)} %get-tuple-element.100) | data formatting | bytes 4194304
  118.6 9.7 %copy.150 = bf16[256,1,4096]{0,2,1:T(8,128)(2,1)} copy(bf16[256,1,4096]{2,1,0:T(2,128)(2,1)} %get-tuple-element.101) | data formatting | bytes 4194304
  128.3 4.6 copy.111
  132.9 5.5 fusion.54
  138.4 1.2 copy.113
  139.6 7.2 %fusion.21 = (f32[256,4,8]{0,2,1:T(8,128)S(1)}, f32[4,512,256,8]{2,1,3,0:T(8,128)}) fusion(pred[256,512]{0,1:T(8,128)(4,1)S(1)} %broadcast_compare_fusion, bf16[256,4,8,128]{0,3,2,1:T(8,128)(2,1)S(1)} %bitcast.150, bf16[512,4,128,1]{2,1,0,3:T(4,128)(2,1)S(1)} %bitcast.157), kind=kOutput, calls=%fused_computation.33 | convolution fusion | flops 1086316544 | bytes 19562496 | tf_op jit(solution)/shard_map/thgd,lhd->thgl/dot_general | solution.py:104
  146.7 36.0 %pmax.14 = f32[256,4,8]{0,2,1:T(8,128)S(1)} all-reduce(f32[256,4,8]{0,2,1:T(8,128)S(1)} %get-tuple-element.105), channel_id=1, replica_groups=mesh['groups'=2,'seq'=8,'head'=2] {'seq'}, use_global_device_ids=true, to_apply=%region_5.6 | all-reduce | flops 8192 | bytes 65536 | tf_op jit(solution)/shard_map/pmax | solution.py:113
  182.8 1.5 multiply_reduce_fusion
  184.3 14.1 %fusion.17 = (f32[256,4,8]{0,2,1:T(8,128)S(1)}, f32[256,4,8]{0,2,1:T(8,128)S(1)}, f32[4,512,256,8]{2,1,3,0:T(8,128)}) fusion(f32[4,512,256,8]{2,1,3,0:T(8,128)} %get-tuple-element.106, f32[256,4,8]{0,2,1:T(8,128)S(1)} %multiply_maximum_fusion, pred[256,512]{0,1:T(8,128)(4,1)S(1)} %broadcast_compare_fusion, bf16[256,4,8,128]{0,3,2,1:T(8,128)(2,1)} %bitcast.154, ...), kind=kOutput, calls=%fused_computation.29 | convolution fusion | flops 1103085568 | bytes 36405248 | tf_op jit(solution)/shard_map/thgd,lhd->thgl/dot_general | solution.py:104
  198.5 34.0 %pmax.15 = f32[256,4,8]{0,2,1:T(8,128)S(1)} all-reduce(f32[256,4,8]{0,2,1:T(8,128)S(1)} %get-tuple-element.77), channel_id=1, replica_groups=mesh['groups'=2,'seq'=8,'head'=2] {'seq'}, use_global_device_ids=true, to_apply=%region_10.11 | all-reduce | flops 8192 | bytes 65536 | tf_op jit(solution)/shard_map/pmax | solution.py:113
  232.7 1.9 fusion.33
  234.8 9.3 %fusion.19 = f32[256,4,8]{0,2,1:T(8,128)S(1)} fusion(f32[4,512,256,8]{2,1,3,0:T(8,128)} %get-tuple-element.107, f32[256,4,8]{0,2,1:T(8,128)S(1)} %max.19, pred[256,512]{0,1:T(8,128)(4,1)S(1)} %broadcast_compare_fusion), kind=kLoop, calls=%fused_computation.31 | loop fusion | flops 16769024 | bytes 16973824 | tf_op jit(solution)/shard_map/reduce_sum | solution.py:140
  244.8 3.1 fusion.35
  247.9 15.8 %bitcast_add_fusion = f32[256,4,8,128]{3,0,2,1:T(8,128)} fusion(f32[256,4,8,128]{3,2,1,0:T(8,128)} %fusion.35, f32[4,512,256,8]{2,1,3,0:T(8,128)} %get-tuple-element.107, f32[256,4,8]{0,2,1:T(8,128)S(1)} %max.19, pred[256,512]{0,1:T(8,128)(4,1)S(1)} %broadcast_compare_fusion, f32[256]{0:T(256)S(1)} %compare_convert_fusion, ...), kind=kOutput, calls=%fused_computation.39 | convolution fusion | flops 1092616192 | bytes 25854976 | tf_op jit(solution)/shard_map/thgl,lhd->thgd/dot_general | solution.py:127
  263.8 10.5 %bitcast_add_fusion.1 = f32[256,4,8,128]{3,0,2,1:T(8,128)} fusion(f32[4,512,256,8]{2,1,3,0:T(8,128)} %get-tuple-element.106, f32[256,4,8]{0,2,1:T(8,128)S(1)} %multiply_maximum_fusion, pred[256,512]{0,1:T(8,128)(4,1)S(1)} %broadcast_compare_fusion, f32[256,4,128]{2,0,1:T(8,128)S(1)} %copy-done.4, f32[256,4,8]{0,2,1:T(8,128)S(1)} %get-tuple-element.103, ...), kind=kOutput, calls=%fused_computation.40 | convolution fusion | flops 1093664768 | bytes 22217728 | tf_op jit(solution)/shard_map/thgl,lhd->thgd/dot_general | solution.py:127
  274.3 6.9 %reshape.162 = bf16[64,64,4,128]{3,2,1,0:T(4,128)(2,1)} reshape(bf16[4096,512]{1,0:T(8,128)(2,1)} %all-gather.4.cloned.1.call-done) | data formatting | bytes 8388608 | tf_op jit(solution)/shard_map/reshape | solution.py:57
  281.2 5.3 copy.176
  286.5 6.9 %reshape.164 = bf16[64,64,4,128]{3,2,1,0:T(4,128)(2,1)} reshape(bf16[4096,512]{1,0:T(8,128)(2,1)} %all-gather.6.cloned.1.call-done) | data formatting | bytes 8388608 | tf_op jit(solution)/shard_map/reshape | solution.py:60
  293.4 5.3 copy.175
  298.7 12.0 %gather_fusion = bf16[640,64,128]{2,1,0:T(8,128)(2,1)} fusion(bf16[4,64,64,128]{3,2,1,0:T(8,128)(2,1)} %bitcast.145, s32[640]{0:T(1024)S(1)} %reshape.173), kind=kCustom, calls=%fused_computation | custom fusion | bytes 20976640 | tf_op jit(solution)/shard_map/gather | solution.py:66
  310.7 11.8 %gather_fusion.1 = bf16[640,64,128]{2,1,0:T(8,128)(2,1)} fusion(bf16[4,64,64,128]{3,2,1,0:T(8,128)(2,1)} %bitcast.146, s32[640]{0:T(1024)S(1)} %reshape.173), kind=kCustom, calls=%fused_computation.1 | custom fusion | bytes 20976640 | tf_op jit(solution)/shard_map/gather | solution.py:67
  322.5 113.4 %while.10 = (s32[]{:T(128)}, bf16[8,64,4,8,128]{4,3,2,1,0:T(8,128)(2,1)}, s32[8,4,20]{2,1,0:T(4,128)S(1)}, s32[8]{0:T(128)S(1)}, bf16[8,4,20,64,128]{4,3,2,1,0:T...) while((s32[]{:T(128)}, ...), condition=%wide.region_3.4_spmd, body=%wide.region_0.3_spmd.sunk | while | flops 1372194048 | bytes 43985448 | solution.py:82
  324.8 2.3 constant_dynamic-slice_fusion.8
  328.2 2.2 fusion.70
  330.4 2.7 fusion.71
  333.1 2.6 fusion.72
  338.9 2.8 constant_dynamic-slice_fusion.8
  342.8 2.2 fusion.70
  345.0 2.7 fusion.71
  347.7 2.6 fusion.72
  353.4 2.3 constant_dynamic-slice_fusion.8
  356.8 2.2 fusion.70
  359.0 2.7 fusion.71
  361.7 2.6 fusion.72
  367.5 2.3 constant_dynamic-slice_fusion.8
  370.8 2.2 fusion.70
  373.0 2.7 fusion.71
  375.8 2.6 fusion.72
  381.5 2.5 constant_dynamic-slice_fusion.8
  385.2 2.2 fusion.70
  387.4 2.7 fusion.71
  390.1 2.6 fusion.72
  395.8 2.3 constant_dynamic-slice_fusion.8
  399.2 2.2 fusion.70
  401.4 2.7 fusion.71
  404.1 2.6 fusion.72
  409.9 2.3 constant_dynamic-slice_fusion.8
  413.2 2.2 fusion.70
  415.4 2.7 fusion.71
  418.2 2.6 fusion.72
  423.9 2.3 constant_dynamic-slice_fusion.8
  427.3 2.2 fusion.70
  429.5 2.7 fusion.71
  432.2 2.6 fusion.72
  435.9 7.4 %reshape.165 = bf16[512,4096]{1,0:T(8,128)(2,1)} reshape(bf16[8,64,4,8,128]{4,3,2,1,0:T(8,128)(2,1)} %get-tuple-element.39) | data formatting | bytes 8388608 | tf_op jit(solution)/shard_map/reshape | solution.py:85
  444.9 160.1 %all-reduce.7.cloned.1.call-done = (f32[256,4,8,128]{3,0,2,1:T(8,128)}, f32[256,4,8,128]{3,0,2,1:T(8,128)}) async-done(((f32[256,4,8,128]{3,0,2,1:T(8,128)}, f32[256,4,8,128]{3,0,2,1:T(8,128)}), (f32[256,4,8,128]{3,0,2,1:T(8,128)}, f32[256,4,8,128]{3,0,2,1:T(8,128)})) %all-reduce.7.cloned.1.call-update) | async-done | bytes 8388624 | tf_op jit(solution)/shard_map/psum | solution.py:143
  605.0 1.6 divide_convert_fusion.1
  607.1 1.3 copy.120
  (167 shorter events, 39.2 us)
Async XLA Ops:
  7.2 76.9 %copy-start = (s32[4,64,20]{1,0,2:T(4,128)S(1)}, s32[4,64,20]{1,0,2:T(4,128)}, u32[]{:S(2)}) copy-start(s32[4,64,20]{1,0,2:T(4,128)} %param.13) | copy-start | bytes 61444
  7.2 43.0 %copy-start.5 = (bf16[32,2,512]{2,1,0:T(2,128)(2,1)S(1)}, bf16[32,2,512]{2,1,0:T(2,128)(2,1)}, u32[]{:S(2)}) copy-start(bf16[32,2,512]{2,1,0:T(2,128)(2,1)} %param.16) | copy-start | bytes 196612
  7.2 90.4 %all-gather.8.cloned.1.call-start = ((), (), s32[]{:S(2)}) async-start(), calls=%async_computation.2 | async-start | bytes 4718592 | tf_op jit(solution)/shard_map/all_gather | solution.py:88
  7.9 266.4 %all-gather.4.cloned.1.call-start = ((), (), s32[]{:S(2)}) async-start(), calls=%async_computation | async-start | bytes 4718592 | tf_op jit(solution)/shard_map/all_gather | solution.py:54
  8.7 277.9 %all-gather.6.cloned.1.call-start = ((), (), s32[]{:S(2)}) async-start(), calls=%async_computation.1 | async-start | bytes 4718592 | tf_op jit(solution)/shard_map/all_gather | solution.py:55
  9.4 433.9 %all-reduce.5.cloned.1.call-start = ((), (), s32[]{:S(2)}) async-start(), calls=%async_computation.3 | async-start | bytes 131072 | tf_op jit(solution)/shard_map/psum | solution.py:143
  82.9 7.2 %copy-start.6 = (s32[256]{0:T(256)S(1)}, s32[256]{0:T(256)}, u32[]{:S(2)}) copy-start(s32[256]{0:T(256)} %param.17) | copy-start | bytes 3076
  184.3 48.4 %copy-start.2 = (f32[256,4,8,2]{2,3,1,0:T(2,128)S(1)}, f32[256,4,8,2]{2,3,1,0:T(2,128)}, u32[]{:S(2)}) copy-start(f32[256,4,8,2]{2,3,1,0:T(2,128)} %get-tuple-element.109) | copy-start | bytes 196612
  244.1 3.8 copy-start.3
  247.9 15.9 %copy-start.4 = (f32[256,4,128]{2,0,1:T(8,128)S(1)}, f32[256,4,128]{2,0,1:T(8,128)}, u32[]{:S(2)}) copy-start(f32[256,4,128]{2,0,1:T(8,128)} %copy.105) | copy-start | bytes 1572868
  263.8 341.2 %all-reduce.7.cloned.1.call-start = ((), (), s32[]{:S(2)}) async-start(), calls=%async_computation.4 | async-start | bytes 16777216 | tf_op jit(solution)/shard_map/psum | solution.py:143
  435.9 172.5 %copy-start.1 = (s32[4,64,20]{1,0,2:T(4,128)S(1)}, s32[4,64,20]{1,0,2:T(4,128)}, u32[]{:S(2)}) copy-start(s32[4,64,20]{1,0,2:T(4,128)} %param.13) | copy-start | bytes 61444
Sparse Core Ops, SparseCore 0:
  10.2 87.3 all-gather.7
  99.7 73.3 all-gather.3
  175.2 72.4 all-gather.5
  263.9 65.9 all-reduce.4
  333.8 271.1 all-reduce.6
where the time goes:
time: 624 us; the launch traced here: 615 us
  waiting for transfers between devices  169 us (27%)
  local copies, waits for them, and re-layouts  152 us (24%)
  blocking collectives  138 us (22%)
  matrix products  94.7 us (15%)
  other arithmetic  40.6 us (7%)
  between operations  14.5 us (2%)
    psum x2, waiting for transfers between devices, local(): mixed, totals = lax.psum((mixed, totals), 'seq')  160 us
    pmax x2, blocking collectives, local(): cache_top = lax.pmax(jnp.max(cache_scores, axis=-1), 'seq')  70 us
    all_gather x1, blocking collectives, local(): lax.all_gather(dec_keys, 'seq', axis=0, tiled=True)  35 us
    all_gather x1, blocking collectives, local(): lax.all_gather(decode_value_rows, 'seq', axis=0, tiled=True)  32.6 us
    dynamic_slice x24, local copies, waits for them, and re-layouts, local(): lax.map(prompt_tile, (blocked_queries, key_matrix, value_matrix, mine.tra...  32.4 us
    dot_general x2, matrix products, local(): jnp.einsum('thgl,lhd->thgd', cache_weights.astype(jnp.bfloat16), cached_v...  26.3 us
    unnamed x19, local copies, waits for them, and re-layouts  26.1 us
    reduce_sum x8, other arithmetic, attend_tile(): total = jnp.sum(weights, axis=-1)  21.7 us
  transfers between devices with their start and end apart: 5, of which 2 were waited for; matrix products, arithmetic and copies ran while one was open for 46% of the time, Pallas kernels for 0%

commit v1 on v0

v1 whole, which is shorter than its diff:
```python
import functools
import math

import jax
import jax.numpy as jnp
from jax import lax
from jax.experimental import pallas as pl
from jax.experimental.pallas import tpu as pltpu
from jax.sharding import PartitionSpec as P

QUERY_HEADS = 64
KEY_VALUE_HEADS = 8
HEAD_SIZE = 128
BLOCK_POSITIONS = 64
DECODE_STEPS = 2
GROUP = QUERY_HEADS // KEY_VALUE_HEADS
FACTOR = math.log2(math.e) / math.sqrt(HEAD_SIZE)
MASKED = -1e30
CHUNK = 4
VMEM_LIMIT = 63 * 1024 * 1024


def ring_orders(n):
    ring = list(range(0, n, 2)) + list(range(n - 1, 0, -2))
    forward = [(ring[i], ring[(i + 1) % n]) for i in range(n)]
    return forward, [(b, a) for a, b in forward]


def wide(x, lanes):
    return jnp.concatenate([x] * (lanes // HEAD_SIZE), axis=1) if lanes > HEAD_SIZE else x[:, :lanes]


def dot_t(a, b):
    return lax.dot_general(a, b, (((1,), (1,)), ((), ())), preferred_element_type=jnp.float32)


def first_part(scores, value_rows):
    top = jnp.broadcast_to(jnp.max(scores, axis=1, keepdims=True), (scores.shape[0], HEAD_SIZE))
    weights = jnp.exp2((scores - wide(top, scores.shape[1])) * FACTOR).astype(jnp.bfloat16)
    both = jnp.concatenate([value_rows, jnp.ones_like(value_rows)], axis=1)
    mixed = jnp.dot(weights, both, preferred_element_type=jnp.float32)
    return top, mixed[:, :HEAD_SIZE], mixed[:, HEAD_SIZE:]


def next_part(scores, value_rows, top, acc, total):
    new_top = jnp.maximum(top, jnp.max(scores, axis=1, keepdims=True))
    weights = jnp.exp2((scores - wide(new_top, scores.shape[1])) * FACTOR).astype(jnp.bfloat16)
    shrink = jnp.exp2((top - new_top) * FACTOR)
    both = jnp.concatenate([value_rows, jnp.ones_like(value_rows)], axis=1)
    mixed = jnp.dot(weights, both, preferred_element_type=jnp.float32)
    return new_top, acc * shrink + mixed[:, :HEAD_SIZE], total * shrink + mixed[:, HEAD_SIZE:]


def stacked_heads(ref, lane):
    parts = [
        ref[:, lane + g * HEAD_SIZE : lane + (g + 1) * HEAD_SIZE] for g in range(GROUP)
    ]
    return jnp.concatenate(parts, axis=0)


def copy_all(pairs, sem):
    copies = [pltpu.make_async_copy(src, dst, sem.at[i]) for i, (src, dst) in enumerate(pairs)]
    for c in copies:
        c.start()
    return copies


def wait_all(copies):
    for c in copies:
        c.wait()


def decode_kernel(lo, shards, heads, first, final, *refs):
    refs = list(refs)
    scal = refs.pop(0)
    q_ref, limit_ref = refs.pop(0), refs.pop(0)
    if first:
        nk_ref, nv_ref = refs.pop(0), refs.pop(0)
    else:
        state_in = refs[:3]
        refs = refs[3:]
    keys, values = refs[:shards], refs[shards : 2 * shards]
    refs = refs[2 * shards :]
    if final:
        out_ref = refs.pop(0)
    else:
        state_out = refs[:3]
        refs = refs[3:]
    key_buf, value_buf, top_ref, acc_ref, total_ref, sem, state_sem = refs
    working = (top_ref, acc_ref, total_ref)
    tokens, length = q_ref.shape[0], keys[0].shape[0]
    lanes = [slice(h * HEAD_SIZE, (h + 1) * HEAD_SIZE) for h in range(heads)]
    spans = [pl.ds(i * length, length) for i in range(shards)]
    if not first:
        state_copies = copy_all(zip(state_in, working), state_sem)
    shard_copies = [
        copy_all(
            ((keys[i], key_buf.at[spans[i], :]), (values[i], value_buf.at[spans[i], :])),
            sem.at[i],
        )
        for i in range(shards)
    ]
    query = [stacked_heads(q_ref, h * GROUP * HEAD_SIZE) for h in range(heads)]
    if first:
        for h in range(heads):
            scores = dot_t(query[h], nk_ref[:, lanes[h]])
            row = lax.broadcasted_iota(jnp.int32, scores.shape, 0) % tokens
            col = lax.broadcasted_iota(jnp.int32, scores.shape, 1)
            allowed = (col <= row) & (col >= row - row % DECODE_STEPS)
            scores = jnp.where(allowed, scores, MASKED)
            top_ref[h], acc_ref[h], total_ref[h] = first_part(scores, nv_ref[:, lanes[h]])
    else:
        wait_all(state_copies)
    for i in range(shards):
        wait_all(shard_copies[i])
        start = scal[2 + lo + i]

        def part(masked, i=i, start=start):
            for h in range(heads):
                scores = dot_t(query[h], key_buf[spans[i], lanes[h]])
                if masked:
                    col = lax.broadcasted_iota(jnp.int32, scores.shape, 1) + start
                    scores = jnp.where(col < wide(limit_ref[...], length), scores, MASKED)
                top_ref[h], acc_ref[h], total_ref[h] = next_part(
                    scores, value_buf[spans[i], lanes[h]], top_ref[h], acc_ref[h], total_ref[h]
                )

        @pl.when(start + length <= scal[0])
        def _():
            part(False)

        @pl.when((start + length > scal[0]) & (start < scal[1]))
        def _():
            part(True)

    if final:
        for h in range(heads):
            result = (acc_ref[h] / total_ref[h]).astype(out_ref.dtype)
            for g in range(GROUP):
                lane = (h * GROUP + g) * HEAD_SIZE
                out_ref[:, lane : lane + HEAD_SIZE] = result[g * tokens : (g + 1) * tokens]
    else:
        wait_all(copy_all(zip(working, state_out), state_sem))


def decode_part(query, limit, scal, keys, values, lo, hi, new=None, state=None, final=False):
    keys, values = keys[lo:hi], values[lo:hi]
    tokens, heads = query.shape[0], keys[0].shape[1] // HEAD_SIZE
    rows, length, shards = tokens * GROUP, keys[0].shape[0], hi - lo
    in_vmem = pl.BlockSpec(memory_space=pltpu.VMEM)
    in_hbm = pl.BlockSpec(memory_space=pltpu.HBM)
    state_shape = jax.ShapeDtypeStruct((heads, rows, HEAD_SIZE), jnp.float32)
    more = list(new) if state is None else list(state)
    in_specs = [in_vmem] * 2 + [in_vmem if state is None else in_hbm] * len(more)
    in_specs += [in_hbm] * (2 * shards)
    if final:
        out_specs, out_shape = in_vmem, jax.ShapeDtypeStruct(query.shape, query.dtype)
    else:
        out_specs, out_shape = [in_hbm] * 3, [state_shape] * 3
    return pl.pallas_call(
        functools.partial(decode_kernel, lo, shards, heads, state is None, final),
        grid_spec=pltpu.PrefetchScalarGridSpec(
            num_scalar_prefetch=1,
            in_specs=in_specs,
            out_specs=out_specs,
            scratch_shapes=[pltpu.VMEM((shards * length, heads * HEAD_SIZE), keys[0].dtype)] * 2
            + [pltpu.VMEM(state_shape.shape, jnp.float32)] * 3
            + [pltpu.SemaphoreType.DMA((shards, 2)), pltpu.SemaphoreType.DMA((3,))],
        ),
        out_shape=out_shape,
        compiler_params=pltpu.CompilerParams(vmem_limit_bytes=VMEM_LIMIT),
        cost_estimate=pl.CostEstimate(
            flops=1, transcendentals=1, bytes_accessed=1
        ),
        name="decode_last" if final else ("decode_first" if state is None else "decode_next"),
    )(scal, query, limit, *more, *keys, *values)


def prompt_kernel(base, lead, shards, heads, slots, first, final, held, *refs):
    refs = list(refs)
    list_ref, count_ref = refs.pop(0), refs.pop(0)
    q_ref = refs.pop(0)
    keys, values = refs[:shards], refs[shards : 2 * shards]
    refs = refs[2 * shards :]
    if not first:
        state_in = refs[:3]
        refs = refs[3:]
    refs = refs[held:]
    if final:
        out_ref = refs.pop(0)
    else:
        working = refs[:3]
        refs = refs[3:]
    key_buf, value_buf, sem = refs[:3]
    if final:
        working = refs[3:]
    length = keys[0].shape[0]

    @pl.when(pl.program_id(0) == 0)
    def _():
        pairs = []
        for i in range(shards):
            at = pl.ds(i * length, length)
            pairs += [(keys[i], key_buf.at[at, :]), (values[i], value_buf.at[at, :])]
        wait_all(copy_all(pairs, sem))

    tile = (pl.program_id(0) + base) * heads
    counts = [count_ref[tile + h] for h in range(heads)]
    most = functools.reduce(jnp.maximum, counts)
    query = [stacked_heads(q_ref, h * GROUP * HEAD_SIZE) for h in range(heads)]

    def chunk(h, at, size):
        lanes = slice(h * HEAD_SIZE, (h + 1) * HEAD_SIZE)
        ks, vs = [], []
        for j in range(size):
            row = list_ref[(tile + h) * slots + at + j] * BLOCK_POSITIONS
            rows = pl.ds(pl.multiple_of(row, BLOCK_POSITIONS), BLOCK_POSITIONS)
            ks.append(key_buf[rows, lanes])
            vs.append(value_buf[rows, lanes])
        scores = dot_t(query[h], jnp.concatenate(ks, axis=0))
        col = lax.broadcasted_iota(jnp.int32, (1, size * BLOCK_POSITIONS), 1)
        bias = jnp.where(col < (counts[h] - at) * BLOCK_POSITIONS, 0.0, MASKED)
        return scores + bias, jnp.concatenate(vs, axis=0)

    def put(h, top, acc, total):
        working[0][h], working[1][h], working[2][h] = top, acc, total

    for h in range(heads):
        scores, value_rows = chunk(h, 0, lead)
        if first:
            row = lax.broadcasted_iota(jnp.int32, (query[h].shape[0], HEAD_SIZE), 0)
            col = lax.broadcasted_iota(jnp.int32, (query[h].shape[0], HEAD_SIZE), 1)
            keep = (col <= row % BLOCK_POSITIONS) | (col >= BLOCK_POSITIONS)
            head_part = jnp.where(keep, scores[:, :HEAD_SIZE], MASKED)
            scores = jnp.concatenate([head_part, scores[:, HEAD_SIZE:]], axis=1)
            put(h, *first_part(scores, value_rows))
        else:
            put(h, *next_part(scores, value_rows, *(ref[h] for ref in state_in)))

    def step(i, carry):
        for h in range(heads):
            scores, value_rows = chunk(h, lead + i * CHUNK, CHUNK)
            put(h, *next_part(scores, value_rows, *(ref[h] for ref in working)))
        return carry

    lax.fori_loop(0, jnp.maximum(most - lead + CHUNK - 1, 0) // CHUNK, step, 0)
    if final:
        for h in range(heads):
            result = (working[1][h] / working[2][h]).astype(out_ref.dtype)
            for g in range(GROUP):
                lane = (h * GROUP + g) * HEAD_SIZE
                rows = slice(g * BLOCK_POSITIONS, (g + 1) * BLOCK_POSITIONS)
                out_ref[:, lane : lane + HEAD_SIZE] = result[rows]


def prompt_part(queries, packed, counts, keys, values, lead, span, state=None, into=None, final=False):
    base, blocks = span[0], span[1] - span[0]
    all_blocks, heads = queries.shape[0] // BLOCK_POSITIONS, keys[0].shape[1] // HEAD_SIZE
    length, shards = keys[0].shape[0], len(keys)
    slots = packed.shape[0] // (all_blocks * heads)
    tile_rows = BLOCK_POSITIONS * GROUP
    row_spec = pl.BlockSpec((BLOCK_POSITIONS, queries.shape[1]), lambda b, *_: (b + base, 0))
    in_hbm = pl.BlockSpec(memory_space=pltpu.HBM)
    state_spec = pl.BlockSpec(
        (None, heads, tile_rows, HEAD_SIZE), lambda b, *_: (b + base, 0, 0, 0)
    )
    state_shape = jax.ShapeDtypeStruct((all_blocks, heads, tile_rows, HEAD_SIZE), jnp.float32)
    in_specs = [row_spec] + [in_hbm] * (2 * shards)
    args = [queries] + list(keys) + list(values)
    if state is not None:
        in_specs += [state_spec] * 3
        args += list(state)
    aliases = {}
    if into is not None:
        aliases = {2 + len(args) + i: i for i in range(3)}
        in_specs += [in_hbm] * 3
        args += list(into)
    scratch = [pltpu.VMEM((shards * length, heads * HEAD_SIZE), keys[0].dtype)] * 2
    scratch += [pltpu.SemaphoreType.DMA((2 * shards,))]
    if final:
        out_specs, out_shape = row_spec, jax.ShapeDtypeStruct(queries.shape, queries.dtype)
        scratch += [pltpu.VMEM((heads, tile_rows, HEAD_SIZE), jnp.float32)] * 3
    else:
        out_specs, out_shape = [state_spec] * 3, [state_shape] * 3
    return pl.pallas_call(
        functools.partial(
            prompt_kernel, base, lead, shards, heads, slots, state is None, final, len(aliases)
        ),
        grid_spec=pltpu.PrefetchScalarGridSpec(
            num_scalar_prefetch=2,
            grid=(blocks,),
            in_specs=in_specs,
            out_specs=out_specs,
            scratch_shapes=scratch,
        ),
        out_shape=out_shape,
        input_output_aliases=aliases,
        compiler_params=pltpu.CompilerParams(vmem_limit_bytes=VMEM_LIMIT),
        cost_estimate=pl.CostEstimate(
            flops=1, transcendentals=1, bytes_accessed=1
        ),
        name="prompt_last" if final else "prompt_first",
    )(packed, counts, *args)


def local(
    n, queries, keys, values, block_lists, dec_queries, dec_keys, decode_value_rows, positions
):
    rows = queries.shape[0]
    per_dev = rows // BLOCK_POSITIONS
    half = n // 2
    me = lax.axis_index("seq")

    def ring_place(s):
        return jnp.where(s % 2 == 0, s // 2, n - 1 - s // 2)

    place = ring_place(me)
    forward, backward = ring_orders(n)
    offsets = [0]
    for d in range(1, half):
        offsets += [-d, d]
    offsets += [half]
    at = (place + jnp.array(offsets, jnp.int32)) % n
    starts = jnp.where(at < half, 2 * at, 2 * (n - 1 - at) + 1) * rows

    first = me * per_dev
    mine = lax.dynamic_slice_in_dim(block_lists, first, per_dev, 1).transpose(1, 0, 2)
    valid = mine >= 0
    entry = jnp.maximum(mine, 0)
    delta = (ring_place(entry // per_dev) - place) % n
    slot = jnp.where(delta < half, 2 * delta, 2 * (n - delta) - 1)
    entry = slot * per_dev + entry % per_dev
    slots = -(-entry.shape[-1] // CHUNK) * CHUNK
    packed = jnp.pad(entry, ((0, 0), (0, 0), (0, slots - entry.shape[-1]))).reshape(-1)
    counts = jnp.sum(valid.astype(jnp.int32), axis=-1).reshape(-1)

    owned, steps = dec_queries.shape[0], dec_queries.shape[1]
    limits = lax.dynamic_slice_in_dim(positions, me * owned, owned, 0)
    query = dec_queries.reshape(owned * steps, -1)
    new = (dec_keys.reshape(owned * steps, -1), decode_value_rows.reshape(owned * steps, -1))
    limit = jnp.broadcast_to(
        limits[None, :, None, None], (GROUP, owned, steps, HEAD_SIZE)
    ).reshape(-1, HEAD_SIZE)
    scal = jnp.concatenate([jnp.min(limits)[None], jnp.max(limits)[None], starts])
    decode = functools.partial(decode_part, query, limit, scal)

    shard_keys, shard_values = [keys], [values]
    key_f, value_f, key_b, value_b = keys, values, keys, values
    before = [None, None]
    for d in range(1, half + 1):
        if before[0] is not None:
            key_f, key_b, before[0] = lax.optimization_barrier((key_f, key_b, before[0]))
        if before[1] is not None:
            value_f, value_b, before[1] = lax.optimization_barrier((value_f, value_b, before[1]))
        key_f = lax.ppermute(key_f, "seq", forward)
        value_b = lax.ppermute(value_b, "seq", backward)
        if d < half:
            key_b = lax.ppermute(key_b, "seq", backward)
            value_f = lax.ppermute(value_f, "seq", forward)
            shard_keys += [key_f, key_b]
            shard_values += [value_f, value_b]
        else:
            shard_keys += [key_f]
            shard_values += [value_b]
        before = [None, None]
        if d == 1:
            state = decode(shard_keys, shard_values, 0, 3, new=new)
        elif d < half - 2:
            state = decode(shard_keys, shard_values, 2 * d - 1, 2 * d + 1, state=state)
            before[1] = state[0]
        elif d == half - 2:
            before[1] = state[0]
    state = decode(shard_keys, shard_values, n - 5, n - 1, state=state)
    decode_out = decode(shard_keys, shard_values, n - 1, n, state=state, final=True)
    prompt_out = prompt_part(
        queries, packed, counts, shard_keys, shard_values, 8, (0, per_dev), final=True
    )
    return prompt_out, decode_out.reshape(owned, steps, -1)


def solution(mesh):
    return jax.shard_map(
        functools.partial(local, mesh.shape["seq"]),
        mesh=mesh,
        in_specs=(
            P(("groups", "seq"), "head"),
            P(("groups", "seq"), "head"),
            P(("groups", "seq"), "head"),
            P("head", "groups", None),
            P(("groups", "seq"), None, "head"),
            P(("groups", "seq"), None, "head"),
            P(("groups", "seq"), None, "head"),
            P("groups"),
        ),
        out_specs=(P(("groups", "seq"), "head"), P(("groups", "seq"), None, "head")),
        check_vma=False,
    )
```

time: 624 us -> 134 us (0.21)
  the two profiles are of different devices: /device:TPU:0 before, /device:TPU:30 now
where the time goes in v1:
time: 134 us; the launch traced here: 133 us
  Pallas kernels  64.2 us (48%)
  waiting for transfers between devices  39.8 us (30%)
  starting transfers between devices  14.3 us (11%)
  local copies, waits for them, and re-layouts  9.89 us (7%)
  other arithmetic  4.16 us (3%)
    pallas_call x1, Pallas kernels, prompt_part(): pl.pallas_call(functools.partial(prompt_kernel, base, lead, shards, heads...  34.1 us
    pallas_call x3, Pallas kernels, decode_part(): pl.pallas_call(functools.partial(decode_kernel, lo, shards, heads, state...  30.1 us
    ppermute x4, waiting for transfers between devices, local(): value_b = lax.ppermute(value_b, 'seq', backward)  22 us
    ppermute x4, waiting for transfers between devices, local(): key_f = lax.ppermute(key_f, 'seq', forward)  9.85 us
    ppermute x3, waiting for transfers between devices, local(): value_f = lax.ppermute(value_f, 'seq', forward)  7.94 us
    ppermute x4, starting transfers between devices, local(): key_f = lax.ppermute(key_f, 'seq', forward)  5.09 us
    ppermute x3, starting transfers between devices, local(): value_f = lax.ppermute(value_f, 'seq', forward)  4.38 us
    ppermute x3, starting transfers between devices, local(): key_b = lax.ppermute(key_b, 'seq', backward)  2.74 us
  transfers between devices with their start and end apart: 14, of which 6 were waited for; matrix products, arithmetic and copies ran while one was open for 9% of the time, Pallas kernels for 18%

profile of v1, /device:TPU:30, one launch (start us, length us, event | category | flops | bytes accessed | tf_op | source)
XLA Modules:
  0.0 133.2 jit_solution(2927184368413041380)
XLA Ops:
  0.6 0.0 copy-start
  0.6 0.6 collective-permute-start.8
  1.2 1.5 %collective-permute-start.7 = (bf16[512,512]{1,0:T(8,128)(2,1)}, bf16[512,512]{1,0:T(8,128)(2,1)}, u32[]{:S(2)}, u32[]{:S(2)}) collective-permute-start(bf16[512,512]{1,0:T(8,128)(2,1)} %refs_11_.1), channel_id=1, source_target_pairs={{0,4},{4,8},{8,12},{12,14},{14,10},{10,6},{6,2},{2,0},{1,5},{5,9},... | collective-permute-start | bytes 1572872 | tf_op jit(solution)/shard_map/ppermute | solution.py:359
  2.7 0.4 collective-permute-start
  3.2 1.6 %collective-permute-start.1 = (bf16[512,512]{1,0:T(8,128)(2,1)}, bf16[512,512]{1,0:T(8,128)(2,1)}, u32[]{:S(2)}, u32[]{:S(2)}) collective-permute-start(bf16[512,512]{1,0:T(8,128)(2,1)} %refs_3_.1), channel_id=1, source_target_pairs={{4,0},{8,4},{12,8},{14,12},{10,14},{6,10},{2,6},{0,2},{5,1},{9,5},... | collective-permute-start | bytes 1572872 | tf_op jit(solution)/shard_map/ppermute | solution.py:358
  4.8 11.0 %collective-permute-done.8.refs_10_.refs_13_ = bf16[512,512]{1,0:T(8,128)(2,1)S(1)} collective-permute-done((bf16[512,512]{1,0:T(8,128)(2,1)}, bf16[512,512]{1,0:T(8,128)(2,1)S(1)}, u32[]{:S(2)}, u32[]{:S(2)}) %collective-permute-start.8) | collective-permute-done | bytes 524320 | tf_op jit(solution)/shard_map/ppermute | solution.py:356
  15.7 0.0 copy-start.1
  15.7 0.5 collective-permute-start.10
  16.3 0.1 collective-permute-done.7.refs_9_.refs_12_
  16.4 1.5 %collective-permute-start.9 = (bf16[512,512]{1,0:T(8,128)(2,1)}, bf16[512,512]{1,0:T(8,128)(2,1)}, u32[]{:S(2)}, u32[]{:S(2)}) collective-permute-start(bf16[512,512]{1,0:T(8,128)(2,1)} %collective-permute-done.7.refs_9_.refs_12_), channel_id=1, source_target_pairs={{0,4},{4,8},{8,12},{12,14},{14,10},{10,6},{6,2},{2,0},{1,5},{5,9},... | collective-permute-start | bytes 1572872 | tf_op jit(solution)/shard_map/ppermute | solution.py:359
  17.9 9.7 %collective-permute-done.refs_6_.refs_4_ = bf16[512,512]{1,0:T(8,128)(2,1)} collective-permute-done((bf16[512,512]{1,0:T(8,128)(2,1)}, bf16[512,512]{1,0:T(8,128)(2,1)}, u32[]{:S(2)}, u32[]{:S(2)}) %collective-permute-start) | collective-permute-done | bytes 524320 | tf_op jit(solution)/shard_map/ppermute | solution.py:355
  27.6 1.5 %collective-permute-start.2 = (bf16[512,512]{1,0:T(8,128)(2,1)}, bf16[512,512]{1,0:T(8,128)(2,1)}, u32[]{:S(2)}, u32[]{:S(2)}) collective-permute-start(bf16[512,512]{1,0:T(8,128)(2,1)} %collective-permute-done.refs_6_.refs_4_), channel_id=1, source_target_pairs={{0,4},{4,8},{8,12},{12,14},{14,10},{10,6},{6,2},{2,0},{1,5},{5,9},... | collective-permute-start | bytes 1572872 | tf_op jit(solution)/shard_map/ppermute | solution.py:355
  29.1 1.5 %fusion.11 = (s32[]{:T(128)}, s32[]{:T(128)}, s32[32]{0:T(128)S(1)}) fusion(s32[256]{0:T(256)} %param.16, s32[]{:T(128)S(6)} %select_n.71), kind=kLoop, calls=%fused_computation.33 | loop fusion | flops 62 | bytes 268 | tf_op jit(solution)/shard_map/reduce_min | solution.py:344
  30.6 0.1 broadcast_in_dim.18
  30.7 0.1 broadcast_in_dim.19
  30.8 2.0 %reshape.27.refs_1_ = bf16[64,4096]{1,0:T(8,128)(2,1)} reshape(bf16[32,2,4096]{2,1,0:T(2,128)(2,1)} %param.13) | data formatting | bytes 1048576 | tf_op jit(solution)/shard_map/reshape | solution.py:339
  32.8 1.5 %reshape.28.refs_3_ = bf16[64,512]{1,0:T(8,128)(2,1)} reshape(bf16[32,2,512]{2,1,0:T(2,128)(2,1)} %param.14) | data formatting | bytes 131072 | tf_op jit(solution)/shard_map/reshape | solution.py:340
  34.3 1.5 %reshape.29.refs_4_ = bf16[64,512]{1,0:T(8,128)(2,1)} reshape(bf16[32,2,512]{2,1,0:T(2,128)(2,1)} %param.15) | data formatting | bytes 131072 | tf_op jit(solution)/shard_map/reshape | solution.py:340
  35.8 0.7 fusion.10
  36.5 1.8 %pad_add_fusion.refs_0_ = s32[10]{0:T(128)} fusion(s32[8]{0:T(128)S(1)} %fusion.10, s32[1]{0:T(128)} %bitcast.5, s32[1]{0:T(128)} %bitcast.4), kind=kLoop, calls=%fused_computation.31 | loop fusion | flops 20 | bytes 80 | tf_op jit(solution)/shard_map/concatenate | solution.py:344
  38.3 0.0 collective-permute-done.1.refs_7_.refs_5_
  38.3 0.5 collective-permute-start.3
  38.9 0.8 broadcast_in_dim.20.refs_2_
  39.7 0.0 copy-done.1
  39.7 10.2 %decode_first.1 = (f32[4,512,128]{2,1,0:T(8,128)}, f32[4,512,128]{2,1,0:T(8,128)}, f32[4,512,128]{2,1,0:T(8,128)}) custom-call(s32[10]{0:T(128)} %pad_add_fusion.refs_0_, bf16[64,4096]{1,0:T(8,128)(2,1)} %reshape.27.refs_1_, s32[512,128]{1,0:T(8,128)} %broadcast_in_dim.20.refs_2_, bf16[64,512]{1,0:T(8,128)(2,1)} %reshape.28.refs_3_, ...), custom_call_target="tpu_custom_call" | custom-call | flops 1 | bytes 1 | tf_op jit(solution)/shard_map/decode_first/pallas_call | solution.py:160
  49.9 0.0 collective-permute-done.10.refs_15_.refs_11_
  49.9 0.0 collective-permute-done.9.refs_14_.refs_10_
  49.9 0.5 collective-permute-start.12
  50.4 0.0 collective-permute-done.2.refs_6_
  50.4 1.6 %collective-permute-start.4 = (bf16[512,512]{1,0:T(8,128)(2,1)}, bf16[512,512]{1,0:T(8,128)(2,1)}, u32[]{:S(2)}, u32[]{:S(2)}) collective-permute-start(bf16[512,512]{1,0:T(8,128)(2,1)} %collective-permute-done.2.refs_6_), channel_id=1, source_target_pairs={{0,4},{4,8},{8,12},{12,14},{14,10},{10,6},{6,2},{2,0},{1,5},{5,9},... | collective-permute-start | bytes 1572872 | tf_op jit(solution)/shard_map/ppermute | solution.py:355
  52.0 1.4 %collective-permute-start.11 = (bf16[512,512]{1,0:T(8,128)(2,1)}, bf16[512,512]{1,0:T(8,128)(2,1)}, u32[]{:S(2)}, u32[]{:S(2)}) collective-permute-start(bf16[512,512]{1,0:T(8,128)(2,1)} %collective-permute-done.9.refs_14_.refs_10_), channel_id=1, source_target_pairs={{0,4},{4,8},{8,12},{12,14},{14,10},{10,6},{6,2},{2,0},{1,5},{5,9},... | collective-permute-start | bytes 1572872 | tf_op jit(solution)/shard_map/ppermute | solution.py:359
  53.4 0.0 collective-permute-done.3.refs_7_
  53.4 0.6 collective-permute-start.5
  54.0 11.0 %collective-permute-done.12.refs_17_.refs_13_ = bf16[512,512]{1,0:T(8,128)(2,1)S(1)} collective-permute-done((bf16[512,512]{1,0:T(8,128)(2,1)}, bf16[512,512]{1,0:T(8,128)(2,1)S(1)}, u32[]{:S(2)}, u32[]{:S(2)}) %collective-permute-start.12) | collective-permute-done | bytes 524320 | tf_op jit(solution)/shard_map/ppermute | solution.py:356
  65.0 0.0 copy-start.2
  65.0 0.5 collective-permute-start.13
  65.5 0.1 collective-permute-done.4.refs_8_
  65.6 1.6 %collective-permute-start.6 = (bf16[512,512]{1,0:T(8,128)(2,1)}, bf16[512,512]{1,0:T(8,128)(2,1)}, u32[]{:S(2)}, u32[]{:S(2)}) collective-permute-start(bf16[512,512]{1,0:T(8,128)(2,1)} %collective-permute-done.4.refs_8_), channel_id=1, source_target_pairs={{0,4},{4,8},{8,12},{12,14},{14,10},{10,6},{6,2},{2,0},{1,5},{5,9},... | collective-permute-start | bytes 1572872 | tf_op jit(solution)/shard_map/ppermute | solution.py:355
  67.1 0.0 copy-done
  67.1 0.1 constant_dynamic-slice_fusion
  67.2 0.1 copy.19
  67.3 0.1 fusion.3
  67.4 0.7 reshape.25.refs_0_
  68.1 0.1 convert_reduce_fusion
  68.2 0.1 copy.17
  68.3 0.7 reshape.26.refs_1_
  69.0 7.8 %collective-permute-done.11.refs_16_.refs_12_ = bf16[512,512]{1,0:T(8,128)(2,1)} collective-permute-done((bf16[512,512]{1,0:T(8,128)(2,1)}, bf16[512,512]{1,0:T(8,128)(2,1)}, u32[]{:S(2)}, u32[]{:S(2)}) %collective-permute-start.11) | collective-permute-done | bytes 524320 | tf_op jit(solution)/shard_map/ppermute | solution.py:359
  76.8 0.0 collective-permute-done.5.refs_9_
  76.8 0.0 copy-done.2
  76.8 13.4 %decode_next.1 = (f32[4,512,128]{2,1,0:T(8,128)}, f32[4,512,128]{2,1,0:T(8,128)}, f32[4,512,128]{2,1,0:T(8,128)}) custom-call(s32[10]{0:T(128)} %pad_add_fusion.refs_0_, bf16[64,4096]{1,0:T(8,128)(2,1)} %reshape.27.refs_1_, s32[512,128]{1,0:T(8,128)} %broadcast_in_dim.20.refs_2_, f32[4,512,128]{2,1,0:T(8,128)} %get-tuple-element.10.refs_3_, ...), custom_call_target="tpu_custom_call" | custom-call | flops 1 | bytes 1 | tf_op jit(solution)/shard_map/decode_next/pallas_call | solution.py:160
  90.2 0.0 collective-permute-done.13.refs_18_.refs_7_
  90.2 0.0 collective-permute-done.6.refs_10_.refs_6_
  90.2 6.5 %decode_last.1 = bf16[64,4096]{1,0:T(8,128)(2,1)} custom-call(s32[10]{0:T(128)} %pad_add_fusion.refs_0_, bf16[64,4096]{1,0:T(8,128)(2,1)} %reshape.27.refs_1_, s32[512,128]{1,0:T(8,128)} %broadcast_in_dim.20.refs_2_, f32[4,512,128]{2,1,0:T(8,128)} %get-tuple-element.15.refs_3_, f32[4,512,128]{2,1,0:T(8,128)} %get-tuple-element.16.refs_4_, ...), custom_call_target="tpu_custom_call" | custom-call | flops 1 | bytes 1 | tf_op jit(solution)/shard_map/decode_last/pallas_call | solution.py:160
  96.8 2.2 %reshape.30 = bf16[32,2,4096]{2,1,0:T(2,128)(2,1)} reshape(bf16[64,4096]{1,0:T(8,128)(2,1)} %decode_last.1) | data formatting | bytes 1048576 | tf_op jit(solution)/shard_map/reshape | solution.py:378
  99.0 34.1 %prompt_last.1 = bf16[512,4096]{1,0:T(8,128)(2,1)} custom-call(s32[640]{0:T(1024)} %reshape.25.refs_0_, s32[32]{0:T(128)} %reshape.26.refs_1_, bf16[512,4096]{1,0:T(8,128)(2,1)} %refs_2_.1, bf16[512,512]{1,0:T(8,128)(2,1)} %refs_3_.1, bf16[512,512]{1,0:T(8,128)(2,1)} %collective-permute-done.refs_6_.refs_4_, ...), custom_call_target="tpu_custom_call" | custom-call | flops 1 | bytes 1 | tf_op jit(solution)/shard_map/prompt_last/pallas_call | solution.py:285
  (1 shorter events, 0.0 us)
Async XLA Ops:
  0.6 66.5 %copy-start = (s32[4,64,20]{1,0,2:T(4,128)S(1)}, s32[4,64,20]{1,0,2:T(4,128)}, u32[]{:S(2)}) copy-start(s32[4,64,20]{1,0,2:T(4,128)} %param.12) | copy-start | bytes 61444
  0.6 15.1 %collective-permute-start.8 = (bf16[512,512]{1,0:T(8,128)(2,1)}, bf16[512,512]{1,0:T(8,128)(2,1)S(1)}, u32[]{:S(2)}, u32[]{:S(2)}) collective-permute-start(bf16[512,512]{1,0:T(8,128)(2,1)} %refs_11_.1), channel_id=1, source_target_pairs={{4,0},{8,4},{12,8},{14,12},{10,14},{6,10},{2,6},{0,2},{5,1},{9,5},... | collective-permute-start | bytes 1572872 | tf_op jit(solution)/shard_map/ppermute | solution.py:356
  1.2 15.2 %collective-permute-start.7 = (bf16[512,512]{1,0:T(8,128)(2,1)}, bf16[512,512]{1,0:T(8,128)(2,1)}, u32[]{:S(2)}, u32[]{:S(2)}) collective-permute-start(bf16[512,512]{1,0:T(8,128)(2,1)} %refs_11_.1), channel_id=1, source_target_pairs={{0,4},{4,8},{8,12},{12,14},{14,10},{10,6},{6,2},{2,0},{1,5},{5,9},... | collective-permute-start | bytes 1572872 | tf_op jit(solution)/shard_map/ppermute | solution.py:359
  2.7 24.9 %collective-permute-start = (bf16[512,512]{1,0:T(8,128)(2,1)}, bf16[512,512]{1,0:T(8,128)(2,1)}, u32[]{:S(2)}, u32[]{:S(2)}) collective-permute-start(bf16[512,512]{1,0:T(8,128)(2,1)} %refs_3_.1), channel_id=1, source_target_pairs={{0,4},{4,8},{8,12},{12,14},{14,10},{10,6},{6,2},{2,0},{1,5},{5,9},... | collective-permute-start | bytes 1572872 | tf_op jit(solution)/shard_map/ppermute | solution.py:355
  3.2 35.1 %collective-permute-start.1 = (bf16[512,512]{1,0:T(8,128)(2,1)}, bf16[512,512]{1,0:T(8,128)(2,1)}, u32[]{:S(2)}, u32[]{:S(2)}) collective-permute-start(bf16[512,512]{1,0:T(8,128)(2,1)} %refs_3_.1), channel_id=1, source_target_pairs={{4,0},{8,4},{12,8},{14,12},{10,14},{6,10},{2,6},{0,2},{5,1},{9,5},... | collective-permute-start | bytes 1572872 | tf_op jit(solution)/shard_map/ppermute | solution.py:358
  15.7 24.0 %copy-start.1 = (bf16[512,512]{1,0:T(8,128)(2,1)}, bf16[512,512]{1,0:T(8,128)(2,1)S(1)}, u32[]{:S(2)}) copy-start(bf16[512,512]{1,0:T(8,128)(2,1)S(1)} %collective-permute-done.8.refs_10_.refs_13_) | copy-start | bytes 1572868
  15.7 34.1 %collective-permute-start.10 = (bf16[512,512]{1,0:T(8,128)(2,1)S(1)}, bf16[512,512]{1,0:T(8,128)(2,1)}, u32[]{:S(2)}, u32[]{:S(2)}) collective-permute-start(bf16[512,512]{1,0:T(8,128)(2,1)S(1)} %collective-permute-done.8.refs_10_.refs_13_), channel_id=1, source_target_pairs={{4,0},{8,4},{12,8},{14,12},{10,14},{6,10},{2,6},{0,2},{5,1},{9,5},... | collective-permute-start | bytes 1572872 | tf_op jit(solution)/shard_map/ppermute | solution.py:356
  16.4 33.5 %collective-permute-start.9 = (bf16[512,512]{1,0:T(8,128)(2,1)}, bf16[512,512]{1,0:T(8,128)(2,1)}, u32[]{:S(2)}, u32[]{:S(2)}) collective-permute-start(bf16[512,512]{1,0:T(8,128)(2,1)} %collective-permute-done.7.refs_9_.refs_12_), channel_id=1, source_target_pairs={{0,4},{4,8},{8,12},{12,14},{14,10},{10,6},{6,2},{2,0},{1,5},{5,9},... | collective-permute-start | bytes 1572872 | tf_op jit(solution)/shard_map/ppermute | solution.py:359
  27.6 22.8 %collective-permute-start.2 = (bf16[512,512]{1,0:T(8,128)(2,1)}, bf16[512,512]{1,0:T(8,128)(2,1)}, u32[]{:S(2)}, u32[]{:S(2)}) collective-permute-start(bf16[512,512]{1,0:T(8,128)(2,1)} %collective-permute-done.refs_6_.refs_4_), channel_id=1, source_target_pairs={{0,4},{4,8},{8,12},{12,14},{14,10},{10,6},{6,2},{2,0},{1,5},{5,9},... | collective-permute-start | bytes 1572872 | tf_op jit(solution)/shard_map/ppermute | solution.py:355
  38.3 15.0 %collective-permute-start.3 = (bf16[512,512]{1,0:T(8,128)(2,1)}, bf16[512,512]{1,0:T(8,128)(2,1)}, u32[]{:S(2)}, u32[]{:S(2)}) collective-permute-start(bf16[512,512]{1,0:T(8,128)(2,1)} %collective-permute-done.1.refs_7_.refs_5_), channel_id=1, source_target_pairs={{4,0},{8,4},{12,8},{14,12},{10,14},{6,10},{2,6},{0,2},{5,1},{9,5},... | collective-permute-start | bytes 1572872 | tf_op jit(solution)/shard_map/ppermute | solution.py:358
  49.9 15.1 %collective-permute-start.12 = (bf16[512,512]{1,0:T(8,128)(2,1)}, bf16[512,512]{1,0:T(8,128)(2,1)S(1)}, u32[]{:S(2)}, u32[]{:S(2)}) collective-permute-start(bf16[512,512]{1,0:T(8,128)(2,1)} %collective-permute-done.10.refs_15_.refs_11_), channel_id=1, source_target_pairs={{4,0},{8,4},{12,8},{14,12},{10,14},{6,10},{2,6},{0,2},{5,1},{9,5},... | collective-permute-start | bytes 1572872 | tf_op jit(solution)/shard_map/ppermute | solution.py:356
  50.4 15.2 %collective-permute-start.4 = (bf16[512,512]{1,0:T(8,128)(2,1)}, bf16[512,512]{1,0:T(8,128)(2,1)}, u32[]{:S(2)}, u32[]{:S(2)}) collective-permute-start(bf16[512,512]{1,0:T(8,128)(2,1)} %collective-permute-done.2.refs_6_), channel_id=1, source_target_pairs={{0,4},{4,8},{8,12},{12,14},{14,10},{10,6},{6,2},{2,0},{1,5},{5,9},... | collective-permute-start | bytes 1572872 | tf_op jit(solution)/shard_map/ppermute | solution.py:355
  52.0 24.8 %collective-permute-start.11 = (bf16[512,512]{1,0:T(8,128)(2,1)}, bf16[512,512]{1,0:T(8,128)(2,1)}, u32[]{:S(2)}, u32[]{:S(2)}) collective-permute-start(bf16[512,512]{1,0:T(8,128)(2,1)} %collective-permute-done.9.refs_14_.refs_10_), channel_id=1, source_target_pairs={{0,4},{4,8},{8,12},{12,14},{14,10},{10,6},{6,2},{2,0},{1,5},{5,9},... | collective-permute-start | bytes 1572872 | tf_op jit(solution)/shard_map/ppermute | solution.py:359
  53.4 23.4 %collective-permute-start.5 = (bf16[512,512]{1,0:T(8,128)(2,1)}, bf16[512,512]{1,0:T(8,128)(2,1)}, u32[]{:S(2)}, u32[]{:S(2)}) collective-permute-start(bf16[512,512]{1,0:T(8,128)(2,1)} %collective-permute-done.3.refs_7_), channel_id=1, source_target_pairs={{4,0},{8,4},{12,8},{14,12},{10,14},{6,10},{2,6},{0,2},{5,1},{9,5},... | collective-permute-start | bytes 1572872 | tf_op jit(solution)/shard_map/ppermute | solution.py:358
  65.0 11.8 %copy-start.2 = (bf16[512,512]{1,0:T(8,128)(2,1)}, bf16[512,512]{1,0:T(8,128)(2,1)S(1)}, u32[]{:S(2)}) copy-start(bf16[512,512]{1,0:T(8,128)(2,1)S(1)} %collective-permute-done.12.refs_17_.refs_13_) | copy-start | bytes 1572868
  65.0 25.2 %collective-permute-start.13 = (bf16[512,512]{1,0:T(8,128)(2,1)S(1)}, bf16[512,512]{1,0:T(8,128)(2,1)}, u32[]{:S(2)}, u32[]{:S(2)}) collective-permute-start(bf16[512,512]{1,0:T(8,128)(2,1)S(1)} %collective-permute-done.12.refs_17_.refs_13_), channel_id=1, source_target_pairs={{4,0},{8,4},{12,8},{14,12},{10,14},{6,10},{2,6},{0,2},{5,1},{9,5},... | collective-permute-start | bytes 1572872 | tf_op jit(solution)/shard_map/ppermute | solution.py:356
  65.6 24.7 %collective-permute-start.6 = (bf16[512,512]{1,0:T(8,128)(2,1)}, bf16[512,512]{1,0:T(8,128)(2,1)}, u32[]{:S(2)}, u32[]{:S(2)}) collective-permute-start(bf16[512,512]{1,0:T(8,128)(2,1)} %collective-permute-done.4.refs_8_), channel_id=1, source_target_pairs={{0,4},{4,8},{8,12},{12,14},{14,10},{10,6},{6,2},{2,0},{1,5},{5,9},... | collective-permute-start | bytes 1572872 | tf_op jit(solution)/shard_map/ppermute | solution.py:355
